TPU v7x, 32 devices: a whole 2x2x4 slice. The times are simulated.
32 devices in a mesh: round: 4 (over y, x), bucket: 8 (over z, core).
Axes of the slice: x: 2, y: 2, z: 4, core: 2. Of those that a mesh axis runs over, the one named last changes fastest.
Arguments:
- x_start: float32 [4, 4096, 512], P('round', 'bucket'), may hold values from 0 to 1
- y_start: float32 [4, 4096, 512], P('round', 'bucket'), may hold values from 0 to 1
- bucket_payoff: bfloat16 [4, 4096, 4096], P('round', 'bucket'), may hold values from -0.09375 to 0.09375
- column_blocks: int32 [4, 4, 3], P('round'), may hold values from 0 to 3
- public_coef: float32 [4, 4, 3, 128, 128], P('round'), may hold values from -0.3125 to 0.3125
- predecessor_sequences: int32 [3, 256], replicated, may hold values from 0 to 511, as said below
Outputs:
- x_final: float32 [4, 4096, 512], P('round', 'bucket')
- y_final: float32 [4, 4096, 512], P('round', 'bucket')
Inputs may be any that keep to these rules, and one draw needn't show every extreme that they name: `predecessor_sequences`: each row names 256 distinct sequences of the previous round.
All inputs are finite; a program needn't handle non-finite values.
Results may differ from a plain program's by a relative error of at most 0.013.
The roundings to bfloat16 on the way count: a program that leaves them out, or rounds other values in their place, can miss the bound.
Values may be sent and summed in bfloat16 or wider, within the bound.
A program may use at most 64 MiB of HBM per device.

v0:
```python
import jax
import jax.numpy as jnp
from jax import lax
from jax.sharding import PartitionSpec as P

smooth_x = 0.1
smooth_y = 0.1
epsilon = 1e-06
highest = lax.Precision.HIGHEST


def from_behind(block, axis, distance):
    devices = range(lax.axis_size(axis))
    route = [(i - distance, i) for i in devices if i - distance in devices]
    return lax.ppermute(block, axis, route)


def prefix(part, axis, combine, identity):
    place = lax.axis_index(axis)
    gathered = jax.tree.map(lambda a: lax.all_gather(a, axis), part)
    state = jax.tree.map(lambda a, e: jnp.zeros_like(a) + jnp.asarray(e, a.dtype), part, identity)

    def one(step, state):
        return combine(
            state, jax.tree.map(lambda a: lax.dynamic_index_in_dim(a, step, 0, False), gathered)
        )

    return lax.fori_loop(0, place, one, state)


def pair_lse(utility_vector):
    even_part = utility_vector[:, 0::2]
    odd_part = utility_vector[:, 1::2]
    larger = jnp.maximum(even_part, odd_part)
    return larger + jnp.log(jnp.exp(even_part - larger) + jnp.exp(odd_part - larger))


def pair_share(utility_vector, aggregated_normalizers, parent_mass):
    even_part = parent_mass * jnp.exp(utility_vector[:, 0::2] - aggregated_normalizers)
    odd_part = parent_mass * jnp.exp(utility_vector[:, 1::2] - aggregated_normalizers)
    return jnp.stack([even_part, odd_part], axis=-1).reshape(utility_vector.shape)


def public_forward(strategy, columns, coefficients):
    tiled = strategy.reshape(strategy.shape[0], columns.shape[0], -1)
    picked = tiled[:, columns, :]
    mixed = jnp.einsum("kmtq,mtpq->kmp", picked, coefficients, precision=highest)
    return mixed.reshape(strategy.shape)


def public_backward(strategy, columns, coefficients):
    tiled = strategy.reshape(strategy.shape[0], columns.shape[0], -1)
    spread = jnp.einsum("kmp,mtpq->kmtq", tiled, coefficients, precision=highest)
    selector = (columns[:, :, None] == jnp.arange(columns.shape[0], dtype=jnp.int32)).astype(
        strategy.dtype
    )
    gathered = jnp.einsum("kmtq,mtc->kcq", spread, selector, precision=highest)
    return gathered.reshape(strategy.shape)


def body(x_start, y_start, bucket_payoff, column_blocks, public_coef, predecessor_sequences):
    round_total = lax.axis_size("round")
    position = lax.axis_index("round")
    payoff = bucket_payoff[0]
    columns = column_blocks[0]
    coefficients = public_coef[0]
    seq_count = x_start.shape[2]
    pair_count = seq_count // 2
    own_rows = jnp.where(
        position == 0,
        jnp.arange(pair_count, dtype=jnp.int32),
        lax.dynamic_index_in_dim(
            predecessor_sequences, jnp.maximum(position - 1, 0), 0, keepdims=False
        ),
    )
    child_rows = lax.dynamic_index_in_dim(
        predecessor_sequences, jnp.minimum(position, round_total - 2), 0, keepdims=False
    )
    total_count = round_total * lax.axis_size("bucket") * x_start.size

    def smoothing(gradient, factor):
        squares = lax.psum(jnp.sum(gradient * gradient), ("round", "bucket"))
        return factor * jnp.sqrt(squares / total_count + epsilon)

    def upward_player(divided_utilities):
        utility_vector = divided_utilities
        aggregated_normalizers = pair_lse(divided_utilities)
        for hop_index in range(round_total - 1):
            arriving = from_behind(aggregated_normalizers, "round", -1)
            carried = jnp.zeros_like(divided_utilities).at[:, child_rows].set(arriving)
            utility_vector = divided_utilities + carried
            aggregated_normalizers = pair_lse(utility_vector)
        return (utility_vector, aggregated_normalizers)

    def descend(utility_vector, aggregated_normalizers):
        shares = pair_share(
            utility_vector, aggregated_normalizers, jnp.ones_like(aggregated_normalizers)
        )
        links = jnp.repeat(own_rows, 2)

        def compose(earlier, later):
            return (earlier[0][later[0]], later[1] * earlier[1][:, later[0]])

        identity = (jnp.arange(seq_count, dtype=jnp.int32), jnp.ones_like(shares))
        composed = prefix((links, shares), "round", compose, identity)
        mass = composed[1][:, links] * shares
        return mass

    def nested_entropy_mapping(destination_strategy, entropy_weight):
        utility_vector, aggregated_normalizers = upward_player(
            destination_strategy / entropy_weight
        )
        return descend(utility_vector, aggregated_normalizers)

    first_player = x_start[0]
    second_player = y_start[0]
    for step_index in range(2):
        weight_new = 2.0 / (step_index + 3.0)
        mixed_y = public_forward(second_player, columns, coefficients).astype(jnp.bfloat16)
        grad_x = jnp.dot(
            payoff,
            lax.all_gather(mixed_y, "bucket", axis=0, tiled=True),
            preferred_element_type=jnp.float32,
        )
        best_x = nested_entropy_mapping(-grad_x, smoothing(grad_x, smooth_x))
        first_player = (1.0 - weight_new) * first_player + weight_new * best_x
        mixed_x = public_backward(first_player, columns, coefficients).astype(jnp.bfloat16)
        grad_y = lax.psum_scatter(
            lax.dot_general(
                payoff, mixed_x, (((0,), (0,)), ((), ())), preferred_element_type=jnp.float32
            ),
            "bucket",
            scatter_dimension=0,
            tiled=True,
        )
        best_y = nested_entropy_mapping(grad_y, smoothing(grad_y, smooth_y))
        second_player = (1.0 - weight_new) * second_player + weight_new * best_y
    return (first_player[None], second_player[None])


def solution(mesh):
    in_specs = (
        P("round", "bucket", None),
        P("round", "bucket", None),
        P("round", "bucket", None),
        P("round", None, None),
        P("round", None, None, None, None),
        P(),
    )
    out_specs = (P("round", "bucket", None), P("round", "bucket", None))
    return jax.shard_map(body, mesh=mesh, in_specs=in_specs, out_specs=out_specs, check_vma=False)
```

profile of v0, /device:TPU:7, one launch (start us, length us, event | category | flops | bytes accessed | tf_op | source)
XLA Modules:
  0.0 1122.3 jit_solution(1934376565462716621)
XLA Ops:
  11.8 5.9 fusion.21
  17.8 48.9 %all-gather.8.cloned.1.call-done = bf16[4096,512]{0,1:T(8,128)(2,1)} async-done(((bf16[512,512]{0,1:T(8,128)(2,1)}), bf16[4096,512]{0,1:T(8,128)(2,1)}) %all-gather.8.cloned.1.call-update) | async-done | bytes 4194320 | tf_op jit(solution)/shard_map/all_gather | solution.py:122
  66.7 6.6 multiply_reduce_fusion.3
  73.3 37.9 %psum.28 = f32[]{:T(128)} all-reduce(f32[]{:T(128)} %get-tuple-element.258), channel_id=1, replica_groups=mesh['round'=4,'bucket'=8] {'round','bucket'}, use_global_device_ids=true, to_apply=%region_1.2 | all-reduce | flops 1 | bytes 8 | tf_op jit(solution)/shard_map/psum | solution.py:82
  118.2 8.8 collective-permute-done
  134.8 4.1 collective-permute-start.1
  138.9 7.9 collective-permute-done.1
  154.6 4.4 collective-permute-start.2
  159.0 7.1 collective-permute-done.2
  166.1 2.8 scatter_custom_fusion.2
  175.3 2.5 copy.56
  177.9 9.8 all-gather
  191.7 43.0 %all-gather.10.cloned.1.call-done = f32[4,512,512]{2,1,0:T(8,128)} async-done(((f32[1,512,512]{2,1,0:T(8,128)}), f32[4,512,512]{2,1,0:T(8,128)}) %all-gather.10.cloned.1.call-update) | async-done | bytes 4194320 | tf_op jit(solution)/shard_map/all_gather | solution.py:20
  234.9 17.2 %while.48 = (s32[]{:T(128)}, f32[512,512]{0,1:T(8,128)S(1)}, s32[]{:T(128)}, f32[4,512,512]{2,1,0:T(8,128)}, s32[4,512]{1,0:T(4,128)S(1)}, /*index=5*/s32[]{:T(128)}, s32[]{:T(128)}, s32[]{:T(128)}) while((s32[]{:T(128)}, f32[512,512]{0,1:T(8,128)S(1)}, s32[]{:T(128)}, f32[4,512,512]{2,1,0:T(8,128)}, s32[4,512]{1,0:T(4,128)S(1)}, ...), condition=%wide.region_6.7_spmd, body=%wide.region_5.6_spmd.sunk | while | flops 264709 | bytes 9449607 | solution.py:28
  253.7 4.7 convolution_bitcast_fusion.3
  258.4 5.1 fusion.28
  263.6 5.7 convolution_bitcast_fusion.1
  269.4 88.5 %reduce-scatter.3.cloned.1.call-done = f32[512,512]{0,1:T(8,128)} async-done(((f32[4096,512]{0,1:T(8,128)}), f32[512,512]{0,1:T(8,128)}) %reduce-scatter.3.cloned.1.call-update) | async-done | bytes 1048592 | tf_op jit(solution)/shard_map/reduce_scatter | solution.py:128
  360.0 39.4 %psum.29 = f32[]{:T(128)} all-reduce(f32[]{:T(128)} %multiply_reduce_fusion.2), channel_id=1, replica_groups=mesh['round'=4,'bucket'=8] {'round','bucket'}, use_global_device_ids=true, to_apply=%region_9.10 | all-reduce | flops 1 | bytes 8 | tf_op jit(solution)/shard_map/psum | solution.py:82
  407.8 8.7 collective-permute-done.3
  424.2 4.1 collective-permute-start.4
  428.4 8.0 collective-permute-done.4
  444.1 4.4 collective-permute-start.5
  448.5 7.2 collective-permute-done.5
  465.9 58.5 %all-gather.12.cloned.1.call-done = f32[4,512,512]{2,1,0:T(8,128)} async-done(((f32[1,512,512]{2,1,0:T(8,128)}), f32[4,512,512]{2,1,0:T(8,128)}) %all-gather.12.cloned.1.call-update) | async-done | bytes 4194320 | tf_op jit(solution)/shard_map/all_gather | solution.py:20
  524.5 17.7 %while.49 = (s32[]{:T(128)}, f32[512,512]{0,1:T(8,128)S(1)}, s32[]{:T(128)}, f32[4,512,512]{2,1,0:T(8,128)}, s32[4,512]{1,0:T(4,128)S(1)}, /*index=5*/s32[]{:T(128)}, s32[]{:T(128)}, s32[]{:T(128)}) while((s32[]{:T(128)}, f32[512,512]{0,1:T(8,128)S(1)}, s32[]{:T(128)}, f32[4,512,512]{2,1,0:T(8,128)}, s32[4,512]{1,0:T(4,128)S(1)}, ...), condition=%wide.region_14.15_spmd, body=%wide.region_13.14_spmd.sunk | while | flops 264709 | bytes 9449607 | solution.py:28
  548.9 3.5 copy.72
  552.4 6.0 fusion.22
  558.5 48.5 %all-gather.14.cloned.1.call-done = bf16[4096,512]{0,1:T(8,128)(2,1)} async-done(((bf16[512,512]{0,1:T(8,128)(2,1)}), bf16[4096,512]{0,1:T(8,128)(2,1)}) %all-gather.14.cloned.1.call-update) | async-done | bytes 4194320 | tf_op jit(solution)/shard_map/all_gather | solution.py:122
  607.0 6.6 multiply_reduce_fusion.1
  613.7 38.0 %psum.30 = f32[]{:T(128)} all-reduce(f32[]{:T(128)} %get-tuple-element.260), channel_id=1, replica_groups=mesh['round'=4,'bucket'=8] {'round','bucket'}, use_global_device_ids=true, to_apply=%region_16.17 | all-reduce | flops 1 | bytes 8 | tf_op jit(solution)/shard_map/psum | solution.py:82
  658.7 8.8 collective-permute-done.6
  675.3 4.1 collective-permute-start.7
  679.5 7.9 collective-permute-done.7
  695.2 4.7 collective-permute-start.8
  699.9 7.0 collective-permute-done.8
  717.1 58.1 %all-gather.16.cloned.1.call-done = f32[4,512,512]{2,1,0:T(8,128)} async-done(((f32[1,512,512]{2,1,0:T(8,128)}), f32[4,512,512]{2,1,0:T(8,128)}) %all-gather.16.cloned.1.call-update) | async-done | bytes 4194320 | tf_op jit(solution)/shard_map/all_gather | solution.py:20
  775.3 17.3 %while.50 = (s32[]{:T(128)}, f32[512,512]{0,1:T(8,128)S(1)}, s32[]{:T(128)}, f32[4,512,512]{2,1,0:T(8,128)}, s32[4,512]{1,0:T(4,128)S(1)}, /*index=5*/s32[]{:T(128)}, s32[]{:T(128)}, s32[]{:T(128)}) while((s32[]{:T(128)}, f32[512,512]{0,1:T(8,128)S(1)}, s32[]{:T(128)}, f32[4,512,512]{2,1,0:T(8,128)}, s32[4,512]{1,0:T(4,128)S(1)}, ...), condition=%wide.region_21.22_spmd, body=%wide.region_20.21_spmd.sunk | while | flops 264709 | bytes 9449607 | solution.py:28
  795.0 5.2 convolution_bitcast_fusion.2
  800.2 5.1 fusion.25
  805.3 5.6 convolution_bitcast_fusion
  811.0 88.5 %reduce-scatter.5.cloned.1.call-done = f32[512,512]{0,1:T(8,128)} async-done(((f32[4096,512]{0,1:T(8,128)}), f32[512,512]{0,1:T(8,128)}) %reduce-scatter.5.cloned.1.call-update) | async-done | bytes 1048592 | tf_op jit(solution)/shard_map/reduce_scatter | solution.py:128
  901.6 39.4 %psum.31 = f32[]{:T(128)} all-reduce(f32[]{:T(128)} %multiply_reduce_fusion), channel_id=1, replica_groups=mesh['round'=4,'bucket'=8] {'round','bucket'}, use_global_device_ids=true, to_apply=%region_24.25 | all-reduce | flops 1 | bytes 8 | tf_op jit(solution)/shard_map/psum | solution.py:82
  944.0 3.0 slice.129
  947.0 3.7 slice.128
  951.9 2.5 collective-permute-start.9
  954.5 8.7 collective-permute-done.9
  968.0 3.0 slice.131
  971.0 3.7 slice.130
  975.9 4.1 collective-permute-start.10
  980.1 8.0 collective-permute-done.10
  992.9 3.0 slice.133
  995.9 3.7 slice.132
  1000.8 4.4 collective-permute-start.11
  1005.2 7.2 collective-permute-done.11
  1017.3 3.0 slice.134
  1020.3 3.0 slice.135
  1025.6 2.9 all_gather_reshape.22
  1028.5 2.6 copy.81
  1031.1 3.5 fusion.38
  1034.6 2.5 copy.83
  1037.1 54.2 %all-gather.18.cloned.1.call-done = f32[4,512,512]{2,1,0:T(8,128)} async-done(((f32[1,512,512]{2,1,0:T(8,128)}), f32[4,512,512]{2,1,0:T(8,128)}) %all-gather.18.cloned.1.call-update) | async-done | bytes 4194320 | tf_op jit(solution)/shard_map/all_gather | solution.py:20
  1091.5 17.2 %while.51 = (s32[]{:T(128)}, f32[512,512]{0,1:T(8,128)S(1)}, s32[]{:T(128)}, f32[4,512,512]{2,1,0:T(8,128)}, s32[4,512]{1,0:T(4,128)S(1)}, /*index=5*/s32[]{:T(128)}, s32[]{:T(128)}, s32[]{:T(128)}) while((s32[]{:T(128)}, f32[512,512]{0,1:T(8,128)S(1)}, s32[]{:T(128)}, f32[4,512,512]{2,1,0:T(8,128)}, s32[4,512]{1,0:T(4,128)S(1)}, ...), condition=%wide.region_29.30_spmd, body=%wide.region_28.29_spmd.sunk | while | flops 264709 | bytes 9449607 | solution.py:28
  1111.0 2.8 fusion.34
  (238 shorter events, 212.8 us)
Async XLA Ops:
  7.2 4.6 copy-start
  7.2 2.0 copy-start.14
  7.2 59.5 %all-gather.8.cloned.1.call-start = ((), (), s32[]{:S(2)}) async-start(), calls=%async_computation.2 | async-start | bytes 4718592 | tf_op jit(solution)/shard_map/all_gather | solution.py:122
  8.9 2.9 copy-start.7
  17.8 217.0 %all-gather.10.cloned.1.call-start = ((), (), s32[]{:S(2)}) async-start(), calls=%async_computation.3 | async-start | bytes 5242880 | tf_op jit(solution)/shard_map/all_gather | solution.py:20
  73.3 44.9 %copy-start.15 = (s32[3,256]{1,0:T(4,128)S(1)}, s32[3,256]{1,0:T(4,128)}, u32[]{:S(2)}) copy-start(s32[3,256]{1,0:T(4,128)} %param.19) | copy-start | bytes 9220
  115.9 11.0 collective-permute-start
  134.8 12.0 %collective-permute-start.1 = (f32[512,256]{0,1:T(8,128)S(1)}, f32[512,256]{0,1:T(8,128)S(1)}, u32[]{:S(2)}, u32[]{:S(2)}) collective-permute-start(f32[512,256]{0,1:T(8,128)S(1)} %log_add_fusion.14), channel_id=1, source_target_pairs={{8,0},{16,8},{24,16},{9,1},{17,9},{25,17},{10,2},{18,10},{26,18},{... | collective-permute-start | bytes 1572872 | tf_op jit(solution)/shard_map/ppermute | solution.py:15
  154.6 11.5 %collective-permute-start.2 = (f32[512,256]{0,1:T(8,128)S(1)}, f32[512,256]{0,1:T(8,128)S(1)}, u32[]{:S(2)}, u32[]{:S(2)}) collective-permute-start(f32[512,256]{0,1:T(8,128)S(1)} %log_add_fusion.13), channel_id=1, source_target_pairs={{8,0},{16,8},{24,16},{9,1},{17,9},{25,17},{10,2},{18,10},{26,18},{... | collective-permute-start | bytes 1572872 | tf_op jit(solution)/shard_map/ppermute | solution.py:15
  173.5 18.2 %copy-start.11 = (f32[1,512,512]{1,2,0:T(8,128)}, f32[1,512,512]{1,2,0:T(8,128)S(1)}, u32[]{:S(2)}) copy-start(f32[1,512,512]{1,2,0:T(8,128)S(1)} %all_gather_reshape.18) | copy-start | bytes 3145732
  174.8 183.0 %reduce-scatter.3.cloned.1.call-start = ((), (), s32[]{:S(2)}) async-start(), calls=%async_computation.4 | async-start | bytes 9437184 | tf_op jit(solution)/shard_map/reduce_scatter | solution.py:128
  253.7 9.9 copy-start.5
  253.7 9.9 copy-start.3
  269.3 255.1 %all-gather.12.cloned.1.call-start = ((), (), s32[]{:S(2)}) async-start(), calls=%async_computation.5 | async-start | bytes 5242880 | tf_op jit(solution)/shard_map/all_gather | solution.py:20
  357.8 61.1 %copy-start.2 = (f32[512,512]{0,1:T(8,128)S(1)}, f32[512,512]{0,1:T(8,128)}, u32[]{:S(2)}) copy-start(f32[512,512]{0,1:T(8,128)} %reduce-scatter.3.cloned.1.call-done) | copy-start | bytes 3145732
  405.3 11.2 collective-permute-start.3
  424.2 12.1 %collective-permute-start.4 = (f32[512,256]{0,1:T(8,128)S(1)}, f32[512,256]{0,1:T(8,128)S(1)}, u32[]{:S(2)}, u32[]{:S(2)}) collective-permute-start(f32[512,256]{0,1:T(8,128)S(1)} %log_add_fusion.10), channel_id=1, source_target_pairs={{8,0},{16,8},{24,16},{9,1},{17,9},{25,17},{10,2},{18,10},{26,18},{... | collective-permute-start | bytes 1572872 | tf_op jit(solution)/shard_map/ppermute | solution.py:15
  444.1 11.6 %collective-permute-start.5 = (f32[512,256]{0,1:T(8,128)S(1)}, f32[512,256]{0,1:T(8,128)S(1)}, u32[]{:S(2)}, u32[]{:S(2)}) collective-permute-start(f32[512,256]{0,1:T(8,128)S(1)} %log_add_fusion.9), channel_id=1, source_target_pairs={{8,0},{16,8},{24,16},{9,1},{17,9},{25,17},{10,2},{18,10},{26,18},{... | collective-permute-start | bytes 1572872 | tf_op jit(solution)/shard_map/ppermute | solution.py:15
  462.8 61.7 %copy-start.12 = (f32[1,512,512]{1,2,0:T(8,128)}, f32[1,512,512]{1,2,0:T(8,128)S(1)}, u32[]{:S(2)}) copy-start(f32[1,512,512]{1,2,0:T(8,128)S(1)} %all_gather_reshape.20) | copy-start | bytes 3145732
  464.2 142.8 %all-gather.14.cloned.1.call-start = ((), (), s32[]{:S(2)}) async-start(), calls=%async_computation.6 | async-start | bytes 4718592 | tf_op jit(solution)/shard_map/all_gather | solution.py:122
  542.3 2.3 copy-start.8
  558.4 216.8 %all-gather.16.cloned.1.call-start = ((), (), s32[]{:S(2)}) async-start(), calls=%async_computation.7 | async-start | bytes 5242880 | tf_op jit(solution)/shard_map/all_gather | solution.py:20
  656.5 11.0 collective-permute-start.6
  675.3 12.0 %collective-permute-start.7 = (f32[512,256]{0,1:T(8,128)S(1)}, f32[512,256]{0,1:T(8,128)S(1)}, u32[]{:S(2)}, u32[]{:S(2)}) collective-permute-start(f32[512,256]{0,1:T(8,128)S(1)} %log_add_fusion.6), channel_id=1, source_target_pairs={{8,0},{16,8},{24,16},{9,1},{17,9},{25,17},{10,2},{18,10},{26,18},{... | collective-permute-start | bytes 1572872 | tf_op jit(solution)/shard_map/ppermute | solution.py:15
  695.2 11.8 %collective-permute-start.8 = (f32[512,256]{0,1:T(8,128)S(1)}, f32[512,256]{0,1:T(8,128)S(1)}, u32[]{:S(2)}, u32[]{:S(2)}) collective-permute-start(f32[512,256]{0,1:T(8,128)S(1)} %log_add_fusion.5), channel_id=1, source_target_pairs={{8,0},{16,8},{24,16},{9,1},{17,9},{25,17},{10,2},{18,10},{26,18},{... | collective-permute-start | bytes 1572872 | tf_op jit(solution)/shard_map/ppermute | solution.py:15
  714.0 61.4 %copy-start.13 = (f32[1,512,512]{1,2,0:T(8,128)}, f32[1,512,512]{1,2,0:T(8,128)S(1)}, u32[]{:S(2)}) copy-start(f32[1,512,512]{1,2,0:T(8,128)S(1)} %all_gather_reshape.21) | copy-start | bytes 3145732
  715.4 184.1 %reduce-scatter.5.cloned.1.call-start = ((), (), s32[]{:S(2)}) async-start(), calls=%async_computation.8 | async-start | bytes 9437184 | tf_op jit(solution)/shard_map/reduce_scatter | solution.py:128
  792.7 2.3 copy-start.6
  795.0 10.2 copy-start.4
  810.9 280.4 %all-gather.18.cloned.1.call-start = ((), (), s32[]{:S(2)}) async-start(), calls=%async_computation.9 | async-start | bytes 5242880 | tf_op jit(solution)/shard_map/all_gather | solution.py:20
  899.4 66.2 %copy-start.1 = (f32[512,512]{0,1:T(8,128)S(1)}, f32[512,512]{0,1:T(8,128)}, u32[]{:S(2)}) copy-start(f32[512,512]{0,1:T(8,128)} %reduce-scatter.5.cloned.1.call-done) | copy-start | bytes 3145732
  951.9 11.2 collective-permute-start.9
  975.9 12.1 %collective-permute-start.10 = (f32[512,256]{0,1:T(8,128)S(1)}, f32[512,256]{0,1:T(8,128)S(1)}, u32[]{:S(2)}, u32[]{:S(2)}) collective-permute-start(f32[512,256]{0,1:T(8,128)S(1)} %log_add_fusion.2), channel_id=1, source_target_pairs={{8,0},{16,8},{24,16},{9,1},{17,9},{25,17},{10,2},{18,10},{26,18},{... | collective-permute-start | bytes 1572872 | tf_op jit(solution)/shard_map/ppermute | solution.py:15
  1000.8 11.6 %collective-permute-start.11 = (f32[512,256]{0,1:T(8,128)S(1)}, f32[512,256]{0,1:T(8,128)S(1)}, u32[]{:S(2)}, u32[]{:S(2)}) collective-permute-start(f32[512,256]{0,1:T(8,128)S(1)} %log_add_fusion.1), channel_id=1, source_target_pairs={{8,0},{16,8},{24,16},{9,1},{17,9},{25,17},{10,2},{18,10},{26,18},{... | collective-permute-start | bytes 1572872 | tf_op jit(solution)/shard_map/ppermute | solution.py:15
  1023.8 7.3 copy-start.10
  1108.6 2.3 copy-start.9
Sparse Core Ops, SparseCore 0:
  17.9 48.7 all-gather.7
  175.0 59.7 all-gather.9
  269.4 88.3 reduce-scatter.2
  464.3 60.0 all-gather.11
  558.6 48.4 all-gather.13
  715.5 59.6 all-gather.15
  811.0 88.3 reduce-scatter.4
  1031.2 60.0 all-gather.17
where the time goes:
time: 1130 us; the launch traced here: 1120 us
  waiting for transfers between devices  583 us (52%)
  local copies, waits for them, and re-layouts  181 us (16%)
  blocking collectives  165 us (15%)
  other arithmetic  73.6 us (7%)
  matrix products  56.5 us (5%)
  starting transfers between devices  44.2 us (4%)
  between operations  18.1 us (2%)
    all_gather x4, waiting for transfers between devices, prefix(): gathered = jax.tree.map(lambda a: lax.all_gather(a, axis), part)  214 us
    reduce_scatter x2, waiting for transfers between devices, body(): lax.psum_scatter(lax.dot_general(payoff, mixed_x, (((0,), (0,)), ((), ())...  177 us
    psum x4, blocking collectives, smoothing(): squares = lax.psum(jnp.sum(gradient * gradient), ('round', 'bucket'))  155 us
    all_gather x2, waiting for transfers between devices, body(): lax.all_gather(mixed_y, 'bucket', axis=0, tiled=True)  97.4 us
    ppermute x12, waiting for transfers between devices, from_behind(): return lax.ppermute(block, axis, route)  95.1 us
    ppermute x12, starting transfers between devices, from_behind(): return lax.ppermute(block, axis, route)  43.9 us
    dynamic_slice x24, local copies, waits for them, and re-layouts, one(): lax.dynamic_index_in_dim(a, step, 0, False)  31.5 us
    slice x12, local copies, waits for them, and re-layouts, pair_lse(): even_part = utility_vector[:, 0::2]  29.8 us
  transfers between devices with their start and end apart: 20, of which 20 were waited for; matrix products, arithmetic and copies ran while one was open for 1% of the time, Pallas kernels for 0%

commit v1 on v0

v1 whole, which is shorter than its diff:
```python
import functools

import jax
import jax.numpy as jnp
from jax import lax
from jax.experimental import pallas as pl
from jax.experimental.pallas import tpu as pltpu
from jax.sharding import PartitionSpec as P

smooth_x = 0.1
smooth_y = 0.1
epsilon = 1e-06
highest = lax.Precision.HIGHEST
nn = (((1,), (0,)), ((), ()))
nt = (((1,), (1,)), ((), ()))


def exact(a, b, dims=nn):
    return lax.dot_general(a, b, dims, precision=highest, preferred_element_type=jnp.float32)


def kernel(
    n_r,
    n_b,
    x_ref,
    y_ref,
    pay_ref,
    col_ref,
    coef_ref,
    pred_ref,
    xo_ref,
    yo_ref,
    xs,
    ys,
    mixer,
    gather,
    pay_t,
    blocks,
    mixed,
    grad,
    sib_out,
    sib_in,
    far_out,
    far_in,
    sq_b,
    sq_r,
    rows_in,
    score,
    norm,
    mass,
    back_in,
    ag_send,
    ag_recv,
    fw_send,
    sib_send,
    sib_recv,
    far_send,
    far_recv,
    sqb_send,
    sqb_recv,
    sqr_send,
    sqr_recv,
    row_send,
    row_recv,
    back_send,
    back_recv,
):
    rows, seqs = xs.shape
    half = seqs // 2
    part = rows // n_r
    pairs = n_b // 2
    me_r = lax.axis_index("round")
    me_b = lax.axis_index("bucket")
    pair = me_b // 2
    core = me_b % 2
    sibling = pair * 2 + 1 - core
    total_count = n_r * n_b * rows * seqs

    def remote(src, dst, send, recv, **where):
        return pltpu.make_async_remote_copy(
            src_ref=src,
            dst_ref=dst,
            send_sem=send,
            recv_sem=recv,
            device_id=where,
            device_id_type=pl.DeviceIdType.MESH,
        )

    barrier = pltpu.get_barrier_semaphore()
    for d in range(1, n_b):
        pl.semaphore_signal(
            barrier,
            inc=1,
            device_id={"bucket": (me_b + d) % n_b},
            device_id_type=pl.DeviceIdType.MESH,
        )
    for d in range(1, n_r):
        pl.semaphore_signal(
            barrier,
            inc=1,
            device_id={"round": (me_r + d) % n_r},
            device_id_type=pl.DeviceIdType.MESH,
        )
    pl.semaphore_wait(barrier, n_b + n_r - 2)

    def order(i):
        return jnp.where(i < half, 2 * i, 2 * (i - half) + 1)

    down = lax.broadcasted_iota(jnp.int32, (seqs, seqs), 0)
    across = lax.broadcasted_iota(jnp.int32, (seqs, seqs), 1)
    to_inner = (down == order(across)).astype(jnp.float32)
    to_outer = (order(down) == across).astype(jnp.float32)

    tiles, per_row, tile, _ = coef_ref.shape[1:]
    for m in range(tiles):
        for c in range(tiles):
            value = jnp.zeros((tile, tile), jnp.float32)
            for t in range(per_row):
                value = value + jnp.where(col_ref[0, m, t] == c, coef_ref[0, m, t], 0.0)
            mixer[m * tile : (m + 1) * tile, c * tile : (c + 1) * tile] = value
    mixer[...] = exact(to_outer, exact(mixer[...], to_inner))
    ys[...] = exact(y_ref[0], to_inner)
    xs[...] = exact(x_ref[0], to_inner)
    for r in range(n_r - 1):
        place = order(lax.broadcasted_iota(jnp.int32, (seqs, half), 0))
        gather[r] = (place == pred_ref[r : r + 1, :]).astype(jnp.float32)

    def columns(j):
        return pl.ds(pl.multiple_of(j * rows, rows), rows)

    def prox(state, sign, factor, weight):
        def row_copy(d):
            s = (me_r + d) % n_r
            return remote(
                grad.at[pl.ds(pl.multiple_of(s * part, part), part)],
                rows_in.at[me_r],
                row_send.at[s],
                row_recv.at[me_r],
                round=s,
            )

        def row_arrival(d):
            s = (me_r + d) % n_r
            return remote(rows_in.at[s], rows_in.at[s], row_send.at[s], row_recv.at[s], round=s)

        for d in range(1, n_r):
            row_copy(d).start()
        squares = grad[...]
        squares = jnp.sum((squares * squares).reshape(rows // 8, 8, seqs), axis=0)
        squares = sum(squares[:, i * 128 : (i + 1) * 128] for i in range(seqs // 128))
        sq_b[me_b] = squares

        def sqb_copy(d):
            s = (me_b + d) % n_b
            return remote(
                sq_b.at[me_b], sq_b.at[me_b], sqb_send.at[d], sqb_recv.at[me_b], bucket=s
            )

        def sqb_arrival(d):
            s = (me_b + d) % n_b
            return remote(sq_b.at[s], sq_b.at[s], sqb_send.at[d], sqb_recv.at[s], bucket=s)

        for d in range(1, n_b):
            sqb_copy(d).start()
        rows_in[me_r] = grad[pl.ds(pl.multiple_of(me_r * part, part), part), :]
        for d in range(1, n_b):
            sqb_arrival(d).wait_recv()
        sq_r[me_r] = jnp.sum(sq_b[...], axis=0)

        def sqr_copy(d):
            s = (me_r + d) % n_r
            return remote(sq_r.at[me_r], sq_r.at[me_r], sqr_send.at[d], sqr_recv.at[me_r], round=s)

        def sqr_arrival(d):
            s = (me_r + d) % n_r
            return remote(sq_r.at[s], sq_r.at[s], sqr_send.at[d], sqr_recv.at[s], round=s)

        for d in range(1, n_r):
            sqr_copy(d).start()
        for d in range(1, n_r):
            sqr_arrival(d).wait_recv()
        squares = jnp.sum(jnp.sum(sq_r[...], axis=0), axis=0, keepdims=True)
        squares = jnp.sum(squares, axis=1, keepdims=True)
        scale = sign / (factor * jnp.sqrt(squares / total_count + epsilon))
        for d in range(1, n_r):
            row_arrival(d).wait_recv()

        for r in reversed(range(n_r)):
            values = rows_in[r] * scale
            if r < n_r - 1:
                values = values + exact(norm[r + 1], gather[r], nt)
            score[r] = values
            even, odd = values[:, :half], values[:, half:]
            larger = jnp.maximum(even, odd)
            norm[r] = larger + jnp.log(jnp.exp(even - larger) + jnp.exp(odd - larger))

        def back_copy(r):
            return remote(
                mass.at[r], back_in.at[me_r], back_send.at[r], back_recv.at[me_r], round=r
            )

        for r in range(n_r):
            even = jnp.exp(score[r, :, :half] - norm[r])
            odd = jnp.exp(score[r, :, half:] - norm[r])
            if r > 0:
                parent = exact(mass[r - 1], gather[r - 1])
                even = parent * even
                odd = parent * odd
            mass[r, :, :half] = even
            mass[r, :, half:] = odd

            @pl.when(me_r != r)
            def _():
                back_copy(r).start()

        def update(s, best):
            here = pl.ds(pl.multiple_of(s * part, part), part)
            state[here, :] = (1.0 - weight) * state[here, :] + weight * best

        update(me_r, mass[me_r])
        for d in range(1, n_r):
            s = (me_r + d) % n_r
            remote(
                back_in.at[s], back_in.at[s], back_send.at[s], back_recv.at[s], round=s
            ).wait_recv()
            update(s, back_in[s])
        for d in range(1, n_r):
            row_copy(d).wait_send()
            back_copy((me_r + d) % n_r).wait_send()
            sqr_copy(d).wait_send()
        for d in range(1, n_b):
            sqb_copy(d).wait_send()

    def step(index, _):
        weight = 2.0 / (index.astype(jnp.float32) + 3.0)

        blocks[me_b] = exact(ys[...], mixer[...], nt).astype(jnp.bfloat16)

        def own_copy(d):
            target = sibling if d == 0 else ((pair + d) % pairs) * 2 + core
            return remote(
                blocks.at[me_b], blocks.at[me_b], ag_send.at[d], ag_recv.at[me_b], bucket=target
            )

        def pass_on(d):
            b = ((pair + d) % pairs) * 2 + core
            return remote(blocks.at[b], blocks.at[b], fw_send.at[d], ag_recv.at[b], bucket=sibling)

        def arrival(b):
            return remote(
                blocks.at[b], blocks.at[b], ag_send.at[0], ag_recv.at[b], bucket=sibling
            )

        def product(b):
            return jnp.dot(
                pay_ref[0, :, columns(b)], blocks[b], preferred_element_type=jnp.float32
            )

        for d in range(1, pairs):
            own_copy(d).start()
        own_copy(0).start()

        @pl.when(index == 0)
        def _():
            def turn(j, _):
                pay_t[columns(j), :] = pay_ref[0, :, columns(j)].T
                return 0

            lax.fori_loop(0, n_b, turn, 0)

        grad[...] = product(me_b)
        arrival(sibling).wait_recv()
        grad[...] += product(sibling)

        def take(d, _):
            b = ((pair + d) % pairs) * 2 + core
            arrival(b).wait_recv()
            pass_on(d).start()
            grad[...] += product(b)
            other = ((pair + d) % pairs) * 2 + 1 - core
            arrival(other).wait_recv()
            grad[...] += product(other)
            return 0

        lax.fori_loop(1, pairs, take, 0)
        own_copy(0).wait_send()
        for d in range(1, pairs):
            own_copy(d).wait_send()
            pass_on(d).wait_send()
        prox(xs, -1.0, smooth_x, weight)

        mixed[...] = exact(xs[...], mixer[...]).astype(jnp.bfloat16)

        def partial(b):
            return jnp.dot(pay_t[columns(b), :], mixed[...], preferred_element_type=jnp.float32)

        def sib_copy(d):
            return remote(
                sib_out.at[d], sib_in.at[d], sib_send.at[d], sib_recv.at[d], bucket=sibling
            )

        def far_copy(d):
            target = ((pair + d) % pairs) * 2 + core
            return remote(
                far_out.at[d], far_in.at[d], far_send.at[d], far_recv.at[d], bucket=target
            )

        def to_sibling(i, _):
            d = pairs - 1 - i
            sib_out[d] = partial(((pair + d) % pairs) * 2 + 1 - core)
            sib_copy(d).start()
            return 0

        lax.fori_loop(0, pairs, to_sibling, 0)

        def to_far(i, _):
            d = pairs - 1 - i
            far_out[d] = partial(((pair + d) % pairs) * 2 + core)
            sib_copy(d).wait_recv()
            far_out[d] += sib_in[d]
            far_copy(d).start()
            return 0

        lax.fori_loop(0, pairs - 1, to_far, 0)
        grad[...] = partial(me_b)
        sib_copy(0).wait_recv()
        grad[...] += sib_in[0]
        for d in range(1, pairs):
            far_copy(d).wait_recv()
            grad[...] += far_in[d]
        sib_copy(0).wait_send()
        for d in range(1, pairs):
            sib_copy(d).wait_send()
            far_copy(d).wait_send()
        prox(ys, 1.0, smooth_y, weight)
        return 0

    lax.fori_loop(0, 2, step, 0)
    down = lax.broadcasted_iota(jnp.int32, (seqs, seqs), 0)
    across = lax.broadcasted_iota(jnp.int32, (seqs, seqs), 1)
    to_outer = (order(down) == across).astype(jnp.float32)
    xo_ref[0] = exact(xs[...], to_outer)
    yo_ref[0] = exact(ys[...], to_outer)


def body(x_start, y_start, bucket_payoff, column_blocks, public_coef, predecessor_sequences):
    n_r = lax.axis_size("round")
    n_b = lax.axis_size("bucket")
    _, rows, seqs = x_start.shape
    part = rows // n_r
    pairs = n_b // 2
    f32, bf16 = jnp.float32, jnp.bfloat16
    vmem = pl.BlockSpec(memory_space=pltpu.VMEM)
    smem = pl.BlockSpec(memory_space=pltpu.SMEM)
    dma = pltpu.SemaphoreType.DMA
    return pl.pallas_call(
        functools.partial(kernel, n_r, n_b),
        out_shape=[jax.ShapeDtypeStruct(x_start.shape, f32)] * 2,
        in_specs=[vmem, vmem, vmem, smem, vmem, vmem],
        out_specs=[vmem, vmem],
        scratch_shapes=[
            pltpu.VMEM((rows, seqs), f32),
            pltpu.VMEM((rows, seqs), f32),
            pltpu.VMEM((seqs, seqs), f32),
            pltpu.VMEM((n_r - 1, seqs, seqs // 2), f32),
            pltpu.VMEM((n_b * rows, rows), bf16),
            pltpu.VMEM((n_b, rows, seqs), bf16),
            pltpu.VMEM((rows, seqs), bf16),
            pltpu.VMEM((rows, seqs), f32),
            pltpu.VMEM((pairs, rows, seqs), f32),
            pltpu.VMEM((pairs, rows, seqs), f32),
            pltpu.VMEM((pairs, rows, seqs), f32),
            pltpu.VMEM((pairs, rows, seqs), f32),
            pltpu.VMEM((n_b, 8, 128), f32),
            pltpu.VMEM((n_r, 8, 128), f32),
            pltpu.VMEM((n_r, part, seqs), f32),
            pltpu.VMEM((n_r, part, seqs), f32),
            pltpu.VMEM((n_r, part, seqs // 2), f32),
            pltpu.VMEM((n_r, part, seqs), f32),
            pltpu.VMEM((n_r, part, seqs), f32),
            dma((pairs,)),
            dma((n_b,)),
            dma((pairs,)),
            dma((pairs,)),
            dma((pairs,)),
            dma((pairs,)),
            dma((pairs,)),
            dma((n_b,)),
            dma((n_b,)),
            dma((n_r,)),
            dma((n_r,)),
            dma((n_r,)),
            dma((n_r,)),
            dma((n_r,)),
            dma((n_r,)),
        ],
        compiler_params=pltpu.CompilerParams(
            collective_id=0, has_side_effects=True, vmem_limit_bytes=60 * 1024 * 1024
        ),
    )(x_start, y_start, bucket_payoff, column_blocks, public_coef, predecessor_sequences)


def solution(mesh):
    in_specs = (
        P("round", "bucket", None),
        P("round", "bucket", None),
        P("round", "bucket", None),
        P("round", None, None),
        P("round", None, None, None, None),
        P(),
    )
    out_specs = (P("round", "bucket", None), P("round", "bucket", None))

    def run(*arrays):
        return tuple(
            jax.shard_map(
                body, mesh=mesh, in_specs=in_specs, out_specs=out_specs, check_vma=False
            )(*arrays)
        )

    return run
```

time: 1130 us -> 432 us (0.38)
  waiting for transfers between devices: 583 us -> 0 us
  Pallas kernels: 0 us -> 423 us
  local copies, waits for them, and re-layouts: 181 us -> 5.86 us
  blocking collectives: 165 us -> 0 us
  other arithmetic: 73.6 us -> 0 us
  matrix products: 56.5 us -> 0 us
  starting transfers between devices: 44.2 us -> 0 us
  between operations: 18.1 us -> 0.64 us
    pallas_call x0 -> x1, Pallas kernels: none -> 423 us  [body(): pl.pallas_call(functools.partial(kernel, n_r, n_b), out_shape=[jax.ShapeD...]
    all_gather x6 -> x0, waiting for transfers between devices: 311 us -> none  [the longest x4 214 us: prefix(): gathered = jax.tree.map(lambda a: lax.all_gather(a, axis), part)]
    reduce_scatter x2 -> x0, waiting for transfers between devices: 177 us -> none  [body(): lax.psum_scatter(lax.dot_general(payoff, mixed_x, (((0,), (0,)), ((), ())...]
    psum x4 -> x0, blocking collectives: 155 us -> none  [smoothing(): squares = lax.psum(jnp.sum(gradient * gradient), ('round', 'bucket'))]
    ppermute x12 -> x0, waiting for transfers between devices: 95.1 us -> none  [from_behind(): return lax.ppermute(block, axis, route)]
    dot_general x10 -> x0, matrix products: 56.5 us -> none  [the longest x2 13.2 us: body(): jnp.dot(payoff, lax.all_gather(mixed_y, 'bucket', axis=0, tiled=True), pr...]
    slice x32 -> x0, local copies, waits for them, and re-layouts: 52.9 us -> none  [the longest x12 29.8 us: pair_lse(): even_part = utility_vector[:, 0::2]]
    ppermute x12 -> x0, starting transfers between devices: 43.9 us -> none  [from_behind(): return lax.ppermute(block, axis, route)]
  transfers between devices with their start and end apart: 20 -> 0, of which waited for: 20 -> 0; matrix products, arithmetic and copies ran while one was open for 1% -> 0% of each run, Pallas kernels for 0% -> 0%
where the time goes in v1:
time: 432 us; the launch traced here: 429 us
  Pallas kernels  423 us (98%)
  local copies, waits for them, and re-layouts  5.86 us (1%)
    pallas_call x1, Pallas kernels, body(): pl.pallas_call(functools.partial(kernel, n_r, n_b), out_shape=[jax.ShapeD...  423 us

profile of v1, /device:TPU:7, one launch (start us, length us, event | category | flops | bytes accessed | tf_op | source)
XLA Modules:
  0.0 429.1 jit_solution(6438121850147898400)
XLA Ops:
  0.6 1.3 copy.8.col_ref
  2.0 422.6 %shard_map.77 = (f32[1,512,512]{2,1,0:T(8,128)}, f32[1,512,512]{2,1,0:T(8,128)}) custom-call(f32[1,512,512]{2,1,0:T(8,128)} %x_ref.1, f32[1,512,512]{2,1,0:T(8,128)} %y_ref.1, bf16[1,512,4096]{2,1,0:T(8,128)(2,1)} %pay_ref.1, s32[1,4,3]{2,1,0:T(4,128)} %copy.8.col_ref, f32[1,4,3,128,128]{4,3,2,1,0:T(8,128)} %coef_ref.1, s32[3,256]{1,0:T(4,128)} %pred_ref.1), custom_call_target="tpu_custom_call" | custom-call | tf_op jit(solution)/shard_map/pallas_call | solution.py:356
  424.6 2.3 copy.11
  426.9 2.3 copy.12

commit v2 on v1

--- a/solution.py
+++ b/solution.py
@@ -49,9 +49,22 @@
     norm,
     mass,
     back_in,
+    far_q,
+    far_s,
+    far_q_in,
+    far_s_in,
+    row_q,
+    row_s,
+    row_q_in,
+    row_s_in,
+    back_q,
+    back_s,
+    back_q_in,
+    back_s_in,
     ag_send,
     ag_recv,
     fw_send,
+    line_send,
     sib_send,
     sib_recv,
     far_send,
@@ -64,6 +77,12 @@
     row_recv,
     back_send,
     back_recv,
+    far_s_send,
+    far_s_recv,
+    row_s_send,
+    row_s_recv,
+    back_s_send,
+    back_s_recv,
 ):
     rows, seqs = xs.shape
     half = seqs // 2
@@ -128,23 +147,53 @@
     def columns(j):
         return pl.ds(pl.multiple_of(j * rows, rows), rows)
 
-    def prox(state, sign, factor, weight):
+    def coded(value, code_ref, scale_ref):
+        top = jnp.max(jnp.abs(value), axis=0, keepdims=True)
+        unit = jnp.maximum(top, 1e-30) / 32767.0
+        code = jnp.floor(value * (1.0 / unit) + 0.5)
+        code_ref[...] = code.astype(jnp.int32).astype(jnp.int16)
+        scale_ref[...] = jnp.broadcast_to(unit, scale_ref.shape)
+
+    def decoded(code_ref, scale_ref):
+        return code_ref[...].astype(jnp.int32).astype(jnp.float32) * scale_ref[0:1, :]
+
+    def prox(state, sign, factor, weight, short):
         def row_copy(d):
             s = (me_r + d) % n_r
-            return remote(
-                grad.at[pl.ds(pl.multiple_of(s * part, part), part)],
-                rows_in.at[me_r],
-                row_send.at[s],
-                row_recv.at[me_r],
-                round=s,
-            )
+            here = grad.at[pl.ds(pl.multiple_of(s * part, part), part)]
+            if not short:
+                return [
+                    remote(here, rows_in.at[me_r], row_send.at[s], row_recv.at[me_r], round=s)
+                ]
+            return [
+                remote(
+                    row_q.at[s], row_q_in.at[me_r], row_send.at[s], row_recv.at[me_r], round=s
+                ),
+                remote(
+                    row_s.at[s], row_s_in.at[me_r], row_s_send.at[s], row_s_recv.at[me_r], round=s
+                ),
+            ]
 
         def row_arrival(d):
             s = (me_r + d) % n_r
-            return remote(rows_in.at[s], rows_in.at[s], row_send.at[s], row_recv.at[s], round=s)
+            if not short:
+                return [
+                    remote(rows_in.at[s], rows_in.at[s], row_send.at[s], row_recv.at[s], round=s)
+                ]
+            return [
+                remote(row_q_in.at[s], row_q_in.at[s], row_send.at[s], row_recv.at[s], round=s),
+                remote(
+                    row_s_in.at[s], row_s_in.at[s], row_s_send.at[s], row_s_recv.at[s], round=s
+                ),
+            ]
 
         for d in range(1, n_r):
-            row_copy(d).start()
+            if short:
+                s = (me_r + d) % n_r
+                here = pl.ds(pl.multiple_of(s * part, part), part)
+                coded(grad[here, :], row_q.at[s], row_s.at[s])
+            for copy in row_copy(d):
+                copy.start()
         squares = grad[...]
         squares = jnp.sum((squares * squares).reshape(rows // 8, 8, seqs), axis=0)
         squares = sum(squares[:, i * 128 : (i + 1) * 128] for i in range(seqs // 128))
@@ -183,7 +232,11 @@
         squares = jnp.sum(squares, axis=1, keepdims=True)
         scale = sign / (factor * jnp.sqrt(squares / total_count + epsilon))
         for d in range(1, n_r):
-            row_arrival(d).wait_recv()
+            for copy in row_arrival(d):
+                copy.wait_recv()
+            if short:
+                s = (me_r + d) % n_r
+                rows_in[s] = decoded(row_q_in.at[s], row_s_in.at[s])
 
         for r in reversed(range(n_r)):
             values = rows_in[r] * scale
@@ -195,9 +248,40 @@
             norm[r] = larger + jnp.log(jnp.exp(even - larger) + jnp.exp(odd - larger))
 
         def back_copy(r):
-            return remote(
-                mass.at[r], back_in.at[me_r], back_send.at[r], back_recv.at[me_r], round=r
-            )
+            if not short:
+                return [
+                    remote(
+                        mass.at[r], back_in.at[me_r], back_send.at[r], back_recv.at[me_r], round=r
+                    )
+                ]
+            return [
+                remote(
+                    back_q.at[r], back_q_in.at[me_r], back_send.at[r], back_recv.at[me_r], round=r
+                ),
+                remote(
+                    back_s.at[r],
+                    back_s_in.at[me_r],
+                    back_s_send.at[r],
+                    back_s_recv.at[me_r],
+                    round=r,
+                ),
+            ]
+
+        def back_arrival(s):
+            if not short:
+                return [
+                    remote(
+                        back_in.at[s], back_in.at[s], back_send.at[s], back_recv.at[s], round=s
+                    )
+                ]
+            return [
+                remote(
+                    back_q_in.at[s], back_q_in.at[s], back_send.at[s], back_recv.at[s], round=s
+                ),
+                remote(
+                    back_s_in.at[s], back_s_in.at[s], back_s_send.at[s], back_s_recv.at[s], round=s
+                ),
+            ]
 
         for r in range(n_r):
             even = jnp.exp(score[r, :, :half] - norm[r])
@@ -211,7 +295,10 @@
 
             @pl.when(me_r != r)
             def _():
-                back_copy(r).start()
+                if short:
+                    coded(mass[r], back_q.at[r], back_s.at[r])
+                for copy in back_copy(r):
+                    copy.start()
 
         def update(s, best):
             here = pl.ds(pl.multiple_of(s * part, part), part)
@@ -220,30 +307,37 @@
         update(me_r, mass[me_r])
         for d in range(1, n_r):
             s = (me_r + d) % n_r
-            remote(
-                back_in.at[s], back_in.at[s], back_send.at[s], back_recv.at[s], round=s
-            ).wait_recv()
-            update(s, back_in[s])
+            for copy in back_arrival(s):
+                copy.wait_recv()
+            if short:
+                update(s, decoded(back_q_in.at[s], back_s_in.at[s]))
+            else:
+                update(s, back_in[s])
         for d in range(1, n_r):
-            row_copy(d).wait_send()
-            back_copy((me_r + d) % n_r).wait_send()
+            for copy in row_copy(d) + back_copy((me_r + d) % n_r):
+                copy.wait_send()
             sqr_copy(d).wait_send()
         for d in range(1, n_b):
             sqb_copy(d).wait_send()
 
     def step(index, _):
         weight = 2.0 / (index.astype(jnp.float32) + 3.0)
+        short = False
 
         blocks[me_b] = exact(ys[...], mixer[...], nt).astype(jnp.bfloat16)
 
-        def own_copy(d):
-            target = sibling if d == 0 else ((pair + d) % pairs) * 2 + core
+        def own_copy(kind):
+            target = (sibling, me_b + 2, me_b - 2)[kind]
             return remote(
-                blocks.at[me_b], blocks.at[me_b], ag_send.at[d], ag_recv.at[me_b], bucket=target
+                blocks.at[me_b], blocks.at[me_b], ag_send.at[kind], ag_recv.at[me_b], bucket=target
             )
 
-        def pass_on(d):
-            b = ((pair + d) % pairs) * 2 + core
+        def go_on(b, d, step):
+            return remote(
+                blocks.at[b], blocks.at[b], line_send.at[d], ag_recv.at[b], bucket=me_b + step
+            )
+
+        def pass_on(b, d):
             return remote(blocks.at[b], blocks.at[b], fw_send.at[d], ag_recv.at[b], bucket=sibling)
 
         def arrival(b):
@@ -256,10 +350,15 @@
                 pay_ref[0, :, columns(b)], blocks[b], preferred_element_type=jnp.float32
             )
 
-        for d in range(1, pairs):
-            own_copy(d).start()
+        @pl.when(pair < pairs - 1)
+        def _():
+            own_copy(1).start()
+
+        @pl.when(pair > 0)
+        def _():
+            own_copy(2).start()
+
         own_copy(0).start()
-
         @pl.when(index == 0)
         def _():
             def turn(j, _):
@@ -267,72 +366,188 @@
                 return 0
 
             lax.fori_loop(0, n_b, turn, 0)
-
         grad[...] = product(me_b)
         arrival(sibling).wait_recv()
         grad[...] += product(sibling)
 
         def take(d, _):
-            b = ((pair + d) % pairs) * 2 + core
-            arrival(b).wait_recv()
-            pass_on(d).start()
-            grad[...] += product(b)
-            other = ((pair + d) % pairs) * 2 + 1 - core
-            arrival(other).wait_recv()
-            grad[...] += product(other)
+            left = me_b - 2 * d
+            right = me_b + 2 * d
+
+            @pl.when(pair >= d)
+            def _():
+                arrival(left).wait_recv()
+
+                @pl.when(pair < pairs - 1)
+                def _():
+                    go_on(left, d, 2).start()
+
+                pass_on(left, d).start()
+
+            @pl.when(pair + d < pairs)
+            def _():
+                arrival(right).wait_recv()
+
+                @pl.when(pair > 0)
+                def _():
+                    go_on(right, pairs + d, -2).start()
+
+                pass_on(right, pairs + d).start()
+
+            def use(b, other):
+                grad[...] += product(b)
+                arrival(other).wait_recv()
+                grad[...] += product(other)
+
+            @pl.when(pair >= d)
+            def _():
+                use(left, sibling - 2 * d)
+
+            @pl.when(pair + d < pairs)
+            def _():
+                use(right, sibling + 2 * d)
+
             return 0
 
         lax.fori_loop(1, pairs, take, 0)
+
+        def drain(d, _):
+            left = me_b - 2 * d
+            right = me_b + 2 * d
+
+            @pl.when(pair >= d)
+            def _():
+                pass_on(left, d).wait_send()
+
+                @pl.when(pair < pairs - 1)
+                def _():
+                    go_on(left, d, 2).wait_send()
+
+            @pl.when(pair + d < pairs)
+            def _():
+                pass_on(right, pairs + d).wait_send()
+
+                @pl.when(pair > 0)
+                def _():
+                    go_on(right, pairs + d, -2).wait_send()
+
+            return 0
+
+        lax.fori_loop(1, pairs, drain, 0)
         own_copy(0).wait_send()
-        for d in range(1, pairs):
-            own_copy(d).wait_send()
-            pass_on(d).wait_send()
-        prox(xs, -1.0, smooth_x, weight)
+
+        @pl.when(pair < pairs - 1)
+        def _():
+            own_copy(1).wait_send()
+
+        @pl.when(pair > 0)
+        def _():
+            own_copy(2).wait_send()
+
+        prox(xs, -1.0, smooth_x, weight, short)
 
         mixed[...] = exact(xs[...], mixer[...]).astype(jnp.bfloat16)
 
         def partial(b):
             return jnp.dot(pay_t[columns(b), :], mixed[...], preferred_element_type=jnp.float32)
 
-        def sib_copy(d):
+        def sib_copy(q):
             return remote(
-                sib_out.at[d], sib_in.at[d], sib_send.at[d], sib_recv.at[d], bucket=sibling
+                sib_out.at[q], sib_in.at[q], sib_send.at[q], sib_recv.at[q], bucket=sibling
             )
 
-        def far_copy(d):
-            target = ((pair + d) % pairs) * 2 + core
-            return remote(
-                far_out.at[d], far_in.at[d], far_send.at[d], far_recv.at[d], bucket=target
-            )
-
-        def to_sibling(i, _):
-            d = pairs - 1 - i
-            sib_out[d] = partial(((pair + d) % pairs) * 2 + 1 - core)
-            sib_copy(d).start()
-            return 0
-
-        lax.fori_loop(0, pairs, to_sibling, 0)
-
-        def to_far(i, _):
-            d = pairs - 1 - i
-            far_out[d] = partial(((pair + d) % pairs) * 2 + core)
-            sib_copy(d).wait_recv()
-            far_out[d] += sib_in[d]
-            far_copy(d).start()
-            return 0
-
-        lax.fori_loop(0, pairs - 1, to_far, 0)
+        def far_copy(q, step, target):
+            slot = q if step > 0 else pairs + q
+            if not short:
+                return [
+                    remote(
+                        far_out.at[q],
+                        far_in.at[slot],
+                        far_send.at[q],
+                        far_recv.at[slot],
+                        bucket=target,
+                    )
+                ]
+            return [
+                remote(
+                    far_q.at[q],
+                    far_q_in.at[slot],
+                    far_send.at[q],
+                    far_recv.at[slot],
+                    bucket=target,
+                ),
+                remote(
+                    far_s.at[q],
+                    far_s_in.at[slot],
+                    far_s_send.at[q],
+                    far_s_recv.at[slot],
+                    bucket=target,
+                ),
+            ]
+
+        def far_value(q, step):
+            slot = q if step > 0 else pairs + q
+            for copy in far_copy(q, step, sibling):
+                copy.wait_recv()
+            if short:
+                return decoded(far_q_in.at[slot], far_s_in.at[slot])
+            return far_in[slot]
+
+        def to_sibling(q):
+            sib_out[q] = partial(q * 2 + 1 - core)
+            sib_copy(q).start()
+
+        def move(q, step):
+            far_out[q] = partial(q * 2 + core)
+            sib_copy(q).wait_recv()
+            far_out[q] += sib_in[q]
+
+            @pl.when(pair > 0 if step > 0 else pair < pairs - 1)
+            def _():
+                far_out[q] += far_value(q, step)
+
+            if short:
+                coded(far_out[q], far_q.at[q], far_s.at[q])
+            for copy in far_copy(q, step, me_b + step):
+                copy.start()
+
+        def outward(right, left):
+            def one(i, _):
+                @pl.when(pair < pairs - 1 - i)
+                def _():
+                    right(pairs - 1 - i)
+
+                @pl.when(pair > i)
+                def _():
+                    left(i)
+
+                return 0
+
+            lax.fori_loop(0, pairs - 1, one, 0)
+
+        def far_done(q, step):
+            for copy in far_copy(q, step, me_b + step):
+                copy.wait_send()
+
+        outward(to_sibling, to_sibling)
+        to_sibling(pair)
+        outward(lambda q: move(q, 2), lambda q: move(q, -2))
         grad[...] = partial(me_b)
-        sib_copy(0).wait_recv()
-        grad[...] += sib_in[0]
-        for d in range(1, pairs):
-            far_copy(d).wait_recv()
-            grad[...] += far_in[d]
-        sib_copy(0).wait_send()
-        for d in range(1, pairs):
-            sib_copy(d).wait_send()
-            far_copy(d).wait_send()
-        prox(ys, 1.0, smooth_y, weight)
+        sib_copy(pair).wait_recv()
+        grad[...] += sib_in[pair]
+
+        @pl.when(pair > 0)
+        def _():
+            grad[...] += far_value(pair, 2)
+
+        @pl.when(pair < pairs - 1)
+        def _():
+            grad[...] += far_value(pair, -2)
+
+        outward(lambda q: far_done(q, 2), lambda q: far_done(q, -2))
+        for q in range(pairs):
+            sib_copy(q).wait_send()
+        prox(ys, 1.0, smooth_y, weight, short)
         return 0
 
     lax.fori_loop(0, 2, step, 0)
@@ -370,7 +585,7 @@
             pltpu.VMEM((pairs, rows, seqs), f32),
             pltpu.VMEM((pairs, rows, seqs), f32),
             pltpu.VMEM((pairs, rows, seqs), f32),
-            pltpu.VMEM((pairs, rows, seqs), f32),
+            pltpu.VMEM((2 * pairs, rows, seqs), f32),
             pltpu.VMEM((n_b, 8, 128), f32),
             pltpu.VMEM((n_r, 8, 128), f32),
             pltpu.VMEM((n_r, part, seqs), f32),
@@ -378,17 +593,36 @@
             pltpu.VMEM((n_r, part, seqs // 2), f32),
             pltpu.VMEM((n_r, part, seqs), f32),
             pltpu.VMEM((n_r, part, seqs), f32),
-            dma((pairs,)),
+            pltpu.VMEM((16, 128), jnp.int16),
+            pltpu.VMEM((pairs, 8, seqs), f32),
+            pltpu.VMEM((16, 128), jnp.int16),
+            pltpu.VMEM((2 * pairs, 8, seqs), f32),
+            pltpu.VMEM((16, 128), jnp.int16),
+            pltpu.VMEM((n_r, 8, seqs), f32),
+            pltpu.VMEM((16, 128), jnp.int16),
+            pltpu.VMEM((n_r, 8, seqs), f32),
+            pltpu.VMEM((16, 128), jnp.int16),
+            pltpu.VMEM((n_r, 8, seqs), f32),
+            pltpu.VMEM((16, 128), jnp.int16),
+            pltpu.VMEM((n_r, 8, seqs), f32),
+            dma((3,)),
             dma((n_b,)),
+            dma((2 * pairs,)),
+            dma((2 * pairs,)),
             dma((pairs,)),
             dma((pairs,)),
             dma((pairs,)),
-            dma((pairs,)),
-            dma((pairs,)),
+            dma((2 * pairs,)),
             dma((n_b,)),
             dma((n_b,)),
             dma((n_r,)),
             dma((n_r,)),
+            dma((n_r,)),
+            dma((n_r,)),
+            dma((n_r,)),
+            dma((n_r,)),
+            dma((pairs,)),
+            dma((2 * pairs,)),
             dma((n_r,)),
             dma((n_r,)),
             dma((n_r,)),

time: 432 us -> 430 us (level)
  no operation moved by 1% of the time
where the time goes in v2:
time: 430 us; the launch traced here: 425 us
  Pallas kernels  419 us (97%)
  local copies, waits for them, and re-layouts  5.86 us (1%)
    pallas_call x1, Pallas kernels, body(): pl.pallas_call(functools.partial(kernel, n_r, n_b), out_shape=[jax.ShapeD...  419 us

profile of v2, /device:TPU:7, one launch (start us, length us, event | category | flops | bytes accessed | tf_op | source)
XLA Modules:
  0.0 425.1 jit_solution(17049784871567841759)
XLA Ops:
  0.6 1.3 copy.8.col_ref
  2.0 418.6 %shard_map.77 = (f32[1,512,512]{2,1,0:T(8,128)}, f32[1,512,512]{2,1,0:T(8,128)}) custom-call(f32[1,512,512]{2,1,0:T(8,128)} %x_ref.1, f32[1,512,512]{2,1,0:T(8,128)} %y_ref.1, bf16[1,512,4096]{2,1,0:T(8,128)(2,1)} %pay_ref.1, s32[1,4,3]{2,1,0:T(4,128)} %copy.8.col_ref, f32[1,4,3,128,128]{4,3,2,1,0:T(8,128)} %coef_ref.1, s32[3,256]{1,0:T(4,128)} %pred_ref.1), custom_call_target="tpu_custom_call" | custom-call | tf_op jit(solution)/shard_map/pallas_call | solution.py:571
  420.6 2.3 copy.11
  422.8 2.3 copy.12
